TPU v7x, 128 devices: a whole 4x4x4 slice. The times are simulated.
128 devices in a mesh: gx: 16 (over z, y), yz: 8 (over x, core).
Axes of the slice: x: 4, y: 4, z: 4, core: 2. Of those that a mesh axis runs over, the one named last changes fastest.
Arguments:
- field: float32 [512, 512, 1024], P('gx', None, 'yz'), may hold values from -58 to 58, as said below
- start: float32 [512, 128], replicated, may hold values from -6 to 6
Outputs:
- basis: float32 [512, 128], replicated
- gram_y: float32 [1024, 1024], P('yz', 'gx')
Inputs may be any that keep to these rules, and one draw needn't show every extreme that they name: `field`: every cell is a real number at most a few tens in magnitude.
All inputs are finite; a program needn't handle non-finite values.
Results may differ from a plain program's by a relative error of at most 0.00025.
Values sent between devices are 32-bit elements; how exact they have to be, the bound alone decides.
A program may use at most 128 MiB of HBM per device.

v0:
```python
import jax
import jax.numpy as jnp
from jax import lax
from jax.sharding import PartitionSpec as P

ITERS = 4


def orthonormal_rows(product, cross):
    lower = lax.linalg.cholesky(cross)
    return lax.linalg.triangular_solve(
        lower, product, left_side=False, lower=True, transpose_a=True
    )


def inner_cross(product):
    return jnp.dot(
        product.T, product, precision=lax.Precision.HIGHEST, preferred_element_type=jnp.float32
    )


def on_device(field, start):
    x_block, depth, y_block = field.shape
    width_y = y_block * lax.axis_size("yz")
    fibres = lax.all_to_all(field, "gx", split_axis=1, concat_axis=0, tiled=True)
    width_x = fibres.shape[0]
    z_local = fibres.shape[1]
    y_local = fibres.shape[2]
    flat = fibres.reshape(width_x, z_local * y_local)
    partial_value = jnp.dot(
        flat, flat.T, precision=lax.Precision.HIGHEST, preferred_element_type=jnp.float32
    )
    total = float(width_y * depth)
    basis = start
    gram_x = lax.psum(partial_value, ("gx", "yz")) / total
    for step in range(ITERS):
        product = jnp.dot(
            gram_x, basis, precision=lax.Precision.HIGHEST, preferred_element_type=jnp.float32
        )
        basis = orthonormal_rows(product, inner_cross(product))
    rank = basis.shape[1]
    core = jnp.dot(
        basis.T, flat, precision=lax.Precision.HIGHEST, preferred_element_type=jnp.float32
    )
    core = core.reshape(rank, z_local, y_local)
    scale = float(rank * depth)
    own_rows = core.reshape(rank * z_local, y_local)
    piece = lax.all_gather(core, "yz", axis=2, tiled=True)
    other = piece.reshape(rank * z_local, piece.shape[2])
    block = jnp.dot(
        own_rows.T, other, precision=lax.Precision.HIGHEST, preferred_element_type=jnp.float32
    )
    gram_y = lax.psum_scatter(block / scale, "gx", scatter_dimension=1, tiled=True)
    return (basis, gram_y)


def solution(mesh):
    placed = (P("gx", None, "yz"), P())
    return jax.shard_map(
        on_device, mesh=mesh, in_specs=placed, out_specs=(P(), P("yz", "gx")), check_vma=False
    )
```

profile of v0, /device:TPU:0, one launch (start us, length us, event | category | flops | bytes accessed | tf_op | source)
XLA Modules:
  0.0 636.2 jit_solution(13347825830865599777)
XLA Ops:
  7.2 8.3 %copy.15 = f32[32,512,128]{2,0,1:T(8,128)S(1)} copy(f32[32,512,128]{2,1,0:T(8,128)} %param.5) | data formatting | bytes 16777216 | tf_op args[0]
  15.5 104.2 %all_to_all.15 = f32[32,512,128]{2,0,1:T(8,128)S(1)} all-to-all(f32[32,512,128]{2,0,1:T(8,128)S(1)} %copy.15), channel_id=1, replica_groups=mesh['gx'=16,'yz'=8] {'gx'}, dimensions={1} | all-to-all | bytes 16777216 | tf_op jit(solution)/shard_map/all_to_all | solution.py:25
  119.7 6.5 %copy.16 = f32[32,16,32,128]{3,2,0,1:T(8,128)S(1)} copy(f32[32,16,32,128]{3,0,2,1:T(8,128)S(1)} %bitcast.77) | data formatting | bytes 16777216 | tf_op jit(solution)/shard_map/all_to_all | solution.py:25
  126.2 3.2 copy-done.1
  129.4 45.5 %fusion.2 = f32[512,512]{1,0:T(8,128)} fusion(f32[64,8,32,128]{3,2,1,0:T(8,128)S(1)} %bitcast.75), kind=kOutput, calls=%fused_computation.2 | convolution fusion | flops 12884901888 | bytes 9437184 | tf_op jit(solution)/shard_map/dot_general | solution.py:30
  175.0 144.3 %all-reduce.2.cloned.1.call-done = f32[512,512]{1,0:T(8,128)} async-done(((f32[512,512]{1,0:T(8,128)}), f32[512,512]{1,0:T(8,128)}) %all-reduce.2.cloned.1.call-update) | async-done | bytes 1048592 | tf_op jit(solution)/shard_map/psum | solution.py:35
  319.3 2.3 fusion.12
  322.3 11.7 %custom-call.12 = f32[128,128]{1,0:T(8,128)S(1)} custom-call(f32[128,128]{1,0:T(8,128)S(1)} %fusion.29), custom_call_target="Cholesky" | custom-call | tf_op jit(solution)/shard_map/cholesky/custom-call.1 | solution.py:10
  334.1 0.6 compare_reduce_fusion.3
  334.7 0.7 fusion.18
  335.4 9.8 %custom-call.13 = f32[1,128,128]{1,2,0:T(8,128)S(1)} custom-call(f32[1,128,128]{2,1,0:T(8,128)S(1)} %fusion.18), custom_call_target="InvertDiagBlocksLowerTriangular" | custom-call | tf_op jit(solution)/shard_map/triangular_solve/custom-call.0 | solution.py:11
  345.6 2.2 fusion.10
  348.5 11.8 %custom-call.14 = f32[128,128]{1,0:T(8,128)S(1)} custom-call(f32[128,128]{1,0:T(8,128)S(1)} %fusion.27), custom_call_target="Cholesky" | custom-call | tf_op jit(solution)/shard_map/cholesky/custom-call.1 | solution.py:10
  360.4 0.6 compare_reduce_fusion.2
  361.1 0.7 fusion.19
  361.7 9.8 %custom-call.15 = f32[1,128,128]{1,2,0:T(8,128)S(1)} custom-call(f32[1,128,128]{2,1,0:T(8,128)S(1)} %fusion.19), custom_call_target="InvertDiagBlocksLowerTriangular" | custom-call | tf_op jit(solution)/shard_map/triangular_solve/custom-call.0 | solution.py:11
  372.0 2.2 fusion.8
  374.9 11.7 %custom-call.16 = f32[128,128]{1,0:T(8,128)S(1)} custom-call(f32[128,128]{1,0:T(8,128)S(1)} %fusion.25), custom_call_target="Cholesky" | custom-call | tf_op jit(solution)/shard_map/cholesky/custom-call.1 | solution.py:10
  387.3 0.7 fusion.20
  387.9 9.8 %custom-call.17 = f32[1,128,128]{1,2,0:T(8,128)S(1)} custom-call(f32[1,128,128]{2,1,0:T(8,128)S(1)} %fusion.20), custom_call_target="InvertDiagBlocksLowerTriangular" | custom-call | tf_op jit(solution)/shard_map/triangular_solve/custom-call.0 | solution.py:11
  398.2 1.2 fusion.6
  400.1 11.7 %custom-call.18 = f32[128,128]{1,0:T(8,128)S(1)} custom-call(f32[128,128]{1,0:T(8,128)S(1)} %fusion.23), custom_call_target="Cholesky" | custom-call | tf_op jit(solution)/shard_map/cholesky/custom-call.1 | solution.py:10
  411.9 0.6 compare_reduce_fusion
  412.5 0.7 fusion.21
  413.2 9.8 %custom-call.19 = f32[1,128,128]{1,2,0:T(8,128)S(1)} custom-call(f32[1,128,128]{2,1,0:T(8,128)S(1)} %fusion.21), custom_call_target="InvertDiagBlocksLowerTriangular" | custom-call | tf_op jit(solution)/shard_map/triangular_solve/custom-call.0 | solution.py:11
  423.4 11.0 %fusion = f32[128,4096]{1,0:T(8,128)S(1)} fusion(f32[512,128]{0,1:T(8,128)S(1)} %convolution_bitcast_fusion, f32[64,8,32,128]{3,2,1,0:T(8,128)} %bitcast.76), kind=kOutput, calls=%fused_computation | convolution fusion | flops 3221225472 | bytes 10747904 | tf_op jit(solution)/shard_map/dot_general | solution.py:42
  434.4 1.7 copy.23
  436.1 1.5 reshape_reshape.3
  437.7 88.1 %all-gather.2.cloned.1.call-done = f32[128,32,1024]{2,1,0:T(8,128)} async-done(((f32[128,32,128]{2,1,0:T(8,128)}), f32[128,32,1024]{2,1,0:T(8,128)}) %all-gather.2.cloned.1.call-update) | async-done | bytes 16777232 | tf_op jit(solution)/shard_map/all_gather | solution.py:48
  525.7 29.9 %convolution_multiply_fusion = f32[128,1024]{0,1:T(8,128)} fusion(f32[4096,128]{1,0:T(8,128)} %reshape_reshape.3, f32[4096,1024]{1,0:T(8,128)} %bitcast.79), kind=kOutput, calls=%fused_computation.6 | convolution fusion | flops 6442582016 | bytes 19398656 | tf_op jit(solution)/shard_map/dot_general | solution.py:50
  555.6 0.8 copy.21
  556.5 72.8 %reduce-scatter.2.cloned.1.call-done = f32[128,64]{0,1:T(8,128)} async-done(((f32[128,1024]{0,1:T(8,128)}), f32[128,64]{0,1:T(8,128)}) %reduce-scatter.2.cloned.1.call-update) | async-done | bytes 32784 | tf_op jit(solution)/shard_map/reduce_scatter | solution.py:53
  (32 shorter events, 5.4 us)
Async XLA Ops:
  7.2 312.1 %copy-start = (f32[512,128]{1,0:T(8,128)S(1)}, f32[512,128]{1,0:T(8,128)}, u32[]{:S(2)}) copy-start(f32[512,128]{1,0:T(8,128)} %param.6) | copy-start | bytes 786436
  7.2 312.1 %all-reduce.2.cloned.1.call-start = ((), (), s32[]{:S(2)}) async-start(), calls=%async_computation.2 | async-start | bytes 2097152 | tf_op jit(solution)/shard_map/psum | solution.py:35
  126.2 3.2 copy-start.1
  175.0 350.8 %all-gather.2.cloned.1.call-start = ((), (), s32[]{:S(2)}) async-start(), calls=%async_computation.3 | async-start | bytes 18874368 | tf_op jit(solution)/shard_map/all_gather | solution.py:48
  319.3 78.9 %copy-start.2 = (f32[512,512]{1,0:T(8,128)S(1)}, f32[512,512]{1,0:T(8,128)}, u32[]{:S(2)}) copy-start(f32[512,512]{1,0:T(8,128)} %all-reduce.2.cloned.1.call-done) | copy-start | bytes 3145732
  436.1 193.2 %reduce-scatter.2.cloned.1.call-start = ((), (), s32[]{:S(2)}) async-start(), calls=%async_computation.4 | async-start | bytes 557056 | tf_op jit(solution)/shard_map/reduce_scatter | solution.py:53
Sparse Core Ops, SparseCore 0:
  175.1 144.1 all-reduce.1
  436.2 89.4 all-gather.1
  555.8 73.4 reduce-scatter.1
where the time goes:
time: 641 us; the launch traced here: 636 us
  waiting for transfers between devices  305 us (48%)
  blocking collectives  104 us (16%)
  matrix products  98.3 us (15%)
  other arithmetic  91.6 us (14%)
  local copies, waits for them, and re-layouts  22.4 us (3%)
  between operations  14.4 us (2%)
    psum x1, waiting for transfers between devices, on_device(): gram_x = lax.psum(partial_value, ('gx', 'yz')) / total  144 us
    all_to_all x1, blocking collectives, on_device(): lax.all_to_all(field, 'gx', split_axis=1, concat_axis=0, tiled=True)  104 us
    all_gather x1, waiting for transfers between devices, on_device(): piece = lax.all_gather(core, 'yz', axis=2, tiled=True)  88.1 us
    reduce_scatter x1, waiting for transfers between devices, on_device(): lax.psum_scatter(block / scale, 'gx', scatter_dimension=1, tiled=True)  72.8 us
    another operation x12, other arithmetic, orthonormal_rows(): lower = lax.linalg.cholesky(cross)  49.7 us
    dot_general x1, matrix products, on_device(): jnp.dot(flat, flat.T, precision=lax.Precision.HIGHEST, preferred_element_...  45.5 us
    another operation x8, other arithmetic, orthonormal_rows(): lax.linalg.triangular_solve(lower, product, left_side=False, lower=True,...  41.9 us
    dot_general x1, matrix products, on_device(): jnp.dot(own_rows.T, other, precision=lax.Precision.HIGHEST, preferred_ele...  29.9 us
  transfers between devices with their start and end apart: 3, of which 3 were waited for; matrix products, arithmetic and copies ran while one was open for 0% of the time, Pallas kernels for 0%

commit v1 on v0

v1 whole, which is shorter than its diff:
```python
import functools

import jax
import jax.numpy as jnp
from jax import lax
from jax.experimental import pallas as pl
from jax.experimental.pallas import tpu as pltpu
from jax.sharding import PartitionSpec as P

ITERS = 4
ROUNDS = 4
RANK = 128
STRIP = 32
F32 = jnp.float32
BF16 = jnp.bfloat16
MESH = pl.DeviceIdType.MESH
NN = (((1,), (0,)), ((), ()))
NT = (((1,), (1,)), ((), ()))
TN = (((0,), (0,)), ((), ()))


def dot(left, right, dims, precision=None):
    return lax.dot_general(left, right, dims, precision=precision, preferred_element_type=F32)


def dot_exact(left, right, dims):
    return dot(left, right, dims, lax.Precision.HIGHEST)


def split(value):
    high = value.astype(BF16)
    return high, (value - high.astype(F32)).astype(BF16)


def split3(value):
    high = value.astype(BF16)
    rest = value - high.astype(F32)
    return (high,) + split(rest)


def position():
    gx, yz = lax.axis_index("gx"), lax.axis_index("yz")
    return gx, yz, gx // 4, gx % 4, yz // 2, yz % 2


def chip_of_step(step):
    gx, yz, z, y, x, c = position()
    sign = 1 + 2 * c
    i, a, b = step % 4, step // 4 % 4, step // 16
    to_z, to_y, to_x = (z + sign * i) % 4, (y + sign * (a + i)) % 4, (x + sign * (b + i)) % 4
    return to_z * 4 + to_y, to_x


def device_of_step(step):
    c = lax.axis_index("yz") % 2
    step = (step + 64 * c) % 128
    to_gx, to_x = chip_of_step(step % 4 + step // 8 * 4)
    return to_gx, to_x * 2 + (c + step // 4) % 2


def each_other_device(action):
    gx, yz = lax.axis_index("gx"), lax.axis_index("yz")

    def body(step, carry):
        to_gx, to_yz = device_of_step(step)

        @pl.when((to_gx != gx) | (to_yz != yz))
        def _():
            action(to_gx, to_yz)

        return carry

    lax.fori_loop(0, 128, body, 0)


def each_other_chip(action):
    c = lax.axis_index("yz") % 2

    def body(step, carry):
        to_gx, to_x = chip_of_step(step)
        action(to_gx, to_x, to_x * 2 + c)
        return carry

    lax.fori_loop(1, 64, body, 0)


def meet_all():
    barrier = pltpu.get_barrier_semaphore()
    each_other_device(
        lambda to_gx, to_yz: pl.semaphore_signal(
            barrier, inc=1, device_id=(to_gx, to_yz), device_id_type=MESH
        )
    )
    pl.semaphore_wait(barrier, 127)


def send_to(src, dst, send_sem, recv_sem, to_gx, to_yz):
    pltpu.make_async_remote_copy(
        src_ref=src,
        dst_ref=dst,
        send_sem=send_sem,
        recv_sem=recv_sem,
        device_id=(to_gx, to_yz),
        device_id_type=MESH,
    ).start()


def wait_for(ref, sem):
    pltpu.make_async_copy(ref, ref, sem).wait()


def reciprocal(value):
    guess = pltpu.reciprocal(value, approx=True)
    guess = guess * (2.0 - value * guess)
    return guess * (2.0 - value * guess)


def inverse_factor(cross):
    n = RANK
    row = lax.broadcasted_iota(jnp.int32, (n, n), 0)
    col = lax.broadcasted_iota(jnp.int32, (n, n), 1)
    eye = row == col
    diagonal = jnp.where(eye, cross, 0.0)
    scale_row = lax.rsqrt(jnp.sum(diagonal, axis=0, keepdims=True))
    scale_col = lax.rsqrt(jnp.sum(diagonal, axis=1, keepdims=True))
    a = cross * scale_row * scale_col
    e = jnp.where(eye, 1.0, 0.0)
    local = lax.broadcasted_iota(jnp.int32, (STRIP, n), 0)
    done = []
    for strip in range(n // STRIP):
        ra = a[STRIP * strip : STRIP * (strip + 1)]
        re = e[STRIP * strip : STRIP * (strip + 1)]
        alpha = jnp.zeros((STRIP, n), F32)
        beta = jnp.zeros((STRIP, n), F32)
        for panel in range(STRIP // 8):
            base = STRIP * strip + 8 * panel
            c = [jnp.broadcast_to(ra[:, base + j : base + j + 1], (STRIP, n)) for j in range(8)]
            for pair in range(4):
                k = 8 * panel + 2 * pair
                c0, c1 = c[2 * pair], c[2 * pair + 1]
                p00, p01, p11 = c0[k : k + 1], c1[k : k + 1], c1[k + 1 : k + 2]
                det = p00 * p11 - p01 * p01
                inv = reciprocal(det)
                below = local > k + 1
                m0 = jnp.where(below, (c0 * p11 - c1 * p01) * inv, 0.0)
                m1 = jnp.where(below, (c1 * p00 - c0 * p01) * inv, 0.0)
                for j in range(2 * pair + 2, 8):
                    c[j] = c[j] - m0 * c[j][k : k + 1] - m1 * c[j][k + 1 : k + 2]
                if k + 2 < STRIP:
                    ra = ra - m0 * ra[k : k + 1] - m1 * ra[k + 1 : k + 2]
                    re = re - m0 * re[k : k + 1] - m1 * re[k + 1 : k + 2]
                s0 = lax.rsqrt(p00)
                s1 = lax.rsqrt(det * (s0 * s0))
                alpha = jnp.where(local == k, s0, jnp.where(local == k + 1, s1, alpha))
                beta = jnp.where(local == k + 1, p01 * (s0 * s0), beta)
        ua = alpha * (ra - beta * pltpu.roll(ra, 1, 0))
        ue = alpha * (re - beta * pltpu.roll(re, 1, 0))
        done.append(ue)
        if strip + 1 < n // STRIP:
            h, m, l = split3(jnp.concatenate([ua, ue], axis=1))
            left = jnp.concatenate([part[:, :n] for part in (h, h, m, h, m, l)], axis=0)
            right = jnp.concatenate([h, m, h, l, m, h], axis=0)
            update = dot(left, right, TN)
            a = a - update[:, :n]
            e = e - update[:, n:]
    return jnp.concatenate(done, axis=0) * scale_row


def kernel(
    field, start, basis, gram_y,
    landed, high, low, both, cross,
    half_gram, pair_gram, sum_gram, parts_gram, all_gram, gram_x,
    core_high, core_low, give, keep, pair_y, parts_y,
    field_send, field_recv, gram_send, gram_recv, y_send, y_recv,
):
    gx, yz, z, y, x, c = position()
    chip = gx * 4 + x
    meet_all()

    own = pl.ds(pl.multiple_of(yz * 512 + gx * 32, 32), 32)
    for r in range(ROUNDS):
        pltpu.make_async_copy(
            field.at[:, (gx * 8 + yz) * ROUNDS + r], landed.at[r, own], field_recv.at[r]
        ).start()
        each_other_device(
            lambda to_gx, to_yz, r=r: send_to(
                field.at[:, (to_gx * 8 + to_yz) * ROUNDS + r],
                landed.at[r, own],
                field_send.at[r],
                field_recv.at[r],
                to_gx,
                to_yz,
            )
        )

    for r in range(ROUNDS):
        wait_for(landed.at[r], field_recv.at[r])
        for j in range(8):
            h, l = split(landed[r, 512 * j : 512 * (j + 1), :])
            high[r, :, 128 * j : 128 * (j + 1)] = h
            low[r, :, 128 * j : 128 * (j + 1)] = l
        h, l = high[r], low[r]
        if r == 0:
            both[...] = dot(h, h, NT)
            cross[...] = dot(h, l, NT)
        else:
            both[...] += dot(h, h, NT)
            cross[...] += dot(h, l, NT)
    for j in range(4):
        columns = slice(128 * j, 128 * (j + 1))
        half_gram[512 * j : 512 * (j + 1), :] = 0.5 * both[:, columns] + cross[:, columns]

    mine = pl.ds(pl.multiple_of(c * 1024, 1024), 1024)
    other = pl.ds(pl.multiple_of((1 - c) * 1024, 1024), 1024)
    partner = x * 2 + 1 - c
    send_to(half_gram.at[other], pair_gram, gram_send.at[0], gram_recv.at[0], gx, partner)
    wait_for(pair_gram, gram_recv.at[0])
    sum_gram[...] = half_gram[mine, :] + pair_gram[...]
    each_other_chip(
        lambda to_gx, to_x, to_yz: send_to(
            sum_gram.at[pl.ds(pl.multiple_of((to_gx * 4 + to_x) * 16, 16), 16)],
            parts_gram.at[chip],
            gram_send.at[1],
            gram_recv.at[1],
            to_gx,
            to_yz,
        )
    )
    parts_gram[chip] = sum_gram[pl.ds(pl.multiple_of(chip * 16, 16), 16), :]
    wait_for(parts_gram.at[pl.ds(0, 63)], gram_recv.at[1])
    piece = pl.ds(pl.multiple_of(c * 1024 + chip * 16, 16), 16)
    all_gram[piece, :] = jnp.sum(parts_gram[...], axis=0)
    each_other_chip(
        lambda to_gx, to_x, to_yz: send_to(
            all_gram.at[piece], all_gram.at[piece], gram_send.at[2], gram_recv.at[2], to_gx, to_yz
        )
    )
    wait_for(all_gram.at[pl.ds(0, 63 * 16)], gram_recv.at[2])
    send_to(all_gram.at[mine], all_gram.at[mine], gram_send.at[3], gram_recv.at[3], gx, partner)
    wait_for(all_gram.at[other], gram_recv.at[3])
    total = jnp.concatenate([all_gram[512 * j : 512 * (j + 1), :] for j in range(4)], axis=1)
    gram_x[...] = (total + total.T) * (1.0 / (512 * 1024))

    basis[...] = start[...]

    def iterate(step, carry):
        product = dot_exact(gram_x[...], basis[...], NN)
        basis[...] = dot_exact(product, inverse_factor(dot_exact(product, product, TN)), NT)
        return carry

    lax.fori_loop(0, ITERS, iterate, 0)

    b_high, b_low = split(basis[...].T)
    for r in range(ROUNDS):
        h, l = high[r], low[r]
        part = dot(b_high, h, NN) + (dot(b_high, l, NN) + dot(b_low, h, NN))
        core_high[RANK * r : RANK * (r + 1), :], core_low[RANK * r : RANK * (r + 1), :] = split(part)

    def columns_of(parity, j):
        at = pl.ds(pl.multiple_of((2 * j + parity) * 128, 128), 128)
        h, l = core_high[:, at], core_low[:, at]
        return dot(core_high[...], h, TN) + (dot(core_high[...], l, TN) + dot(core_low[...], h, TN))

    for j in range(4):
        give[j] = columns_of(1 - c, j)
        send_to(give.at[j], pair_y.at[j], y_send.at[j], y_recv.at[j], gx, partner)
    for j in range(4):
        keep[j] = columns_of(c, j)
    for j in range(4):
        wait_for(pair_y.at[j], y_recv.at[j])
        keep[j] = keep[j] + pair_y[j]

    def piece_y(to_gx, to_x):
        return keep.at[to_x, pl.ds(pl.multiple_of(to_gx * 64, 64), 64)]

    each_other_chip(
        lambda to_gx, to_x, to_yz: send_to(
            piece_y(to_gx, to_x), parts_y.at[chip], y_send.at[4], y_recv.at[4], to_gx, to_yz
        )
    )
    parts_y[chip] = piece_y(gx, x)[...]
    wait_for(parts_y.at[pl.ds(0, 63)], y_recv.at[4])
    gram_y[...] = (jnp.sum(parts_y[...], axis=0) * (1.0 / 65536)).T

    for r in range(ROUNDS):
        wait_for(landed.at[r, pl.ds(0, 127 * 32)], field_send.at[r])
    wait_for(pair_gram, gram_send.at[0])
    wait_for(parts_gram.at[pl.ds(0, 63)], gram_send.at[1])
    wait_for(parts_gram.at[pl.ds(0, 63)], gram_send.at[2])
    wait_for(all_gram.at[mine], gram_send.at[3])
    for j in range(4):
        wait_for(give.at[j], y_send.at[j])
    wait_for(parts_y.at[pl.ds(0, 63)], y_send.at[4])


def on_device(field, start):
    vmem = pl.BlockSpec(memory_space=pltpu.VMEM)
    return pl.pallas_call(
        kernel,
        out_shape=(
            jax.ShapeDtypeStruct((512, RANK), F32),
            jax.ShapeDtypeStruct((128, 64), F32),
        ),
        in_specs=[pl.BlockSpec(memory_space=pl.ANY), vmem],
        out_specs=(vmem, vmem),
        scratch_shapes=[
            pltpu.VMEM((ROUNDS, 4096, 128), F32),
            pltpu.VMEM((ROUNDS, 512, 1024), BF16),
            pltpu.VMEM((ROUNDS, 512, 1024), BF16),
            pltpu.VMEM((512, 512), F32),
            pltpu.VMEM((512, 512), F32),
            pltpu.VMEM((2048, 128), F32),
            pltpu.VMEM((1024, 128), F32),
            pltpu.VMEM((1024, 128), F32),
            pltpu.VMEM((64, 16, 128), F32),
            pltpu.VMEM((2048, 128), F32),
            pltpu.VMEM((512, 512), F32),
            pltpu.VMEM((512, 1024), BF16),
            pltpu.VMEM((512, 1024), BF16),
            pltpu.VMEM((4, 1024, 128), F32),
            pltpu.VMEM((4, 1024, 128), F32),
            pltpu.VMEM((4, 1024, 128), F32),
            pltpu.VMEM((64, 64, 128), F32),
            pltpu.SemaphoreType.DMA((ROUNDS,)),
            pltpu.SemaphoreType.DMA((ROUNDS,)),
            pltpu.SemaphoreType.DMA((4,)),
            pltpu.SemaphoreType.DMA((4,)),
            pltpu.SemaphoreType.DMA((5,)),
            pltpu.SemaphoreType.DMA((5,)),
        ],
        compiler_params=pltpu.CompilerParams(
            collective_id=0, has_side_effects=True, vmem_limit_bytes=56 << 20
        ),
    )(field, start)


def solution(mesh):
    placed = (P("gx", None, "yz"), P())
    return jax.shard_map(
        on_device, mesh=mesh, in_specs=placed, out_specs=(P(), P("yz", "gx")), check_vma=False
    )
```

time: 641 us -> 209 us (0.33)
  waiting for transfers between devices: 305 us -> 0 us
  Pallas kernels: 0 us -> 203 us
  blocking collectives: 104 us -> 0 us
  matrix products: 98.3 us -> 0 us
  other arithmetic: 91.6 us -> 0 us
  local copies, waits for them, and re-layouts: 22.4 us -> 3.21 us
  between operations: 14.4 us -> 0.64 us
    pallas_call x0 -> x1, Pallas kernels: none -> 203 us  [on_device(): pl.pallas_call(kernel, out_shape=(jax.ShapeDtypeStruct((512, RANK), F32),...]
    psum x1 -> x0, waiting for transfers between devices: 144 us -> none  [on_device(): gram_x = lax.psum(partial_value, ('gx', 'yz')) / total]
    all_to_all x1 -> x0, blocking collectives: 104 us -> none  [on_device(): lax.all_to_all(field, 'gx', split_axis=1, concat_axis=0, tiled=True)]
    dot_general x11 -> x0, matrix products: 96.7 us -> none  [the longest x1 45.5 us: on_device(): jnp.dot(flat, flat.T, precision=lax.Precision.HIGHEST, preferred_element_...]
    another operation x20 -> x0, other arithmetic: 91.6 us -> none  [the longest x12 49.7 us: orthonormal_rows(): lower = lax.linalg.cholesky(cross)]
    all_gather x1 -> x0, waiting for transfers between devices: 88.1 us -> none  [on_device(): piece = lax.all_gather(core, 'yz', axis=2, tiled=True)]
    reduce_scatter x1 -> x0, waiting for transfers between devices: 72.8 us -> none  [on_device(): lax.psum_scatter(block / scale, 'gx', scatter_dimension=1, tiled=True)]
    unnamed x9 -> x1, local copies, waits for them, and re-layouts: 14 us -> 1.67 us
  transfers between devices with their start and end apart: 3 -> 0, of which waited for: 3 -> 0; matrix products, arithmetic and copies ran while one was open for 0% -> 0% of each run, Pallas kernels for 0% -> 0%
where the time goes in v1:
time: 209 us; the launch traced here: 207 us
  Pallas kernels  203 us (97%)
  local copies, waits for them, and re-layouts  3.21 us (2%)
    pallas_call x1, Pallas kernels, on_device(): pl.pallas_call(kernel, out_shape=(jax.ShapeDtypeStruct((512, RANK), F32),...  203 us

profile of v1, /device:TPU:0, one launch (start us, length us, event | category | flops | bytes accessed | tf_op | source)
XLA Modules:
  0.0 207.2 jit_solution(12869759300846327286)
XLA Ops:
  0.6 203.4 %shard_map.41 = (f32[512,128]{1,0:T(8,128)}, f32[128,64]{1,0:T(8,128)}) custom-call(f32[32,512,128]{2,1,0:T(8,128)} %field.1, f32[512,128]{1,0:T(8,128)} %start.1), custom_call_target="tpu_custom_call" | custom-call | tf_op jit(solution)/shard_map/pallas_call | solution.py:298
  204.0 1.5 copy.4
  205.6 1.7 copy.6

commit v2 on v1

--- a/solution.py
+++ b/solution.py
@@ -11,6 +11,7 @@
 ROUNDS = 4
 RANK = 128
 STRIP = 32
+PANEL = 16
 F32 = jnp.float32
 BF16 = jnp.bfloat16
 MESH = pl.DeviceIdType.MESH
@@ -43,45 +44,36 @@
     return gx, yz, gx // 4, gx % 4, yz // 2, yz % 2
 
 
-def chip_of_step(step):
+def routes():
     gx, yz, z, y, x, c = position()
     sign = 1 + 2 * c
-    i, a, b = step % 4, step // 4 % 4, step // 16
-    to_z, to_y, to_x = (z + sign * i) % 4, (y + sign * (a + i)) % 4, (x + sign * (b + i)) % 4
-    return to_z * 4 + to_y, to_x
-
-
-def device_of_step(step):
+    to_z, to_y, to_x = ([(at + sign * i) % 4 for i in range(4)] for at in (z, y, x))
+    return [[to_z[i] * 4 + to_y[j] for j in range(4)] for i in range(4)], to_x
+
+
+CHIP_STEPS = [(i, (a + i) % 4, (b + i) % 4) for b in range(4) for a in range(4) for i in range(4)]
+
+
+def each_other_device(action):
+    to_gx, to_x = routes()
     c = lax.axis_index("yz") % 2
-    step = (step + 64 * c) % 128
-    to_gx, to_x = chip_of_step(step % 4 + step // 8 * 4)
-    return to_gx, to_x * 2 + (c + step // 4) % 2
-
-
-def each_other_device(action):
-    gx, yz = lax.axis_index("gx"), lax.axis_index("yz")
-
-    def body(step, carry):
-        to_gx, to_yz = device_of_step(step)
-
-        @pl.when((to_gx != gx) | (to_yz != yz))
-        def _():
-            action(to_gx, to_yz)
-
-        return carry
-
-    lax.fori_loop(0, 128, body, 0)
+    to_x = [jnp.where(c == 0, to_x[i], to_x[(i + 2) % 4]) for i in range(4)]
+    to_yz = [[2 * at + c for at in to_x], [2 * at + 1 - c for at in to_x]]
+    for group in range(16):
+        for flip in range(2):
+            for i, j, k in CHIP_STEPS[4 * group : 4 * group + 4]:
+                act = functools.partial(action, to_gx[i][j], to_yz[flip][k])
+                if (i, j, k % 2, flip) == (0, 0, 0, 0):
+                    pl.when(c != k // 2)(act)
+                else:
+                    act()
 
 
 def each_other_chip(action):
+    to_gx, to_x = routes()
     c = lax.axis_index("yz") % 2
-
-    def body(step, carry):
-        to_gx, to_x = chip_of_step(step)
-        action(to_gx, to_x, to_x * 2 + c)
-        return carry
-
-    lax.fori_loop(1, 64, body, 0)
+    for i, j, k in CHIP_STEPS[1:]:
+        action(to_gx[i][j], to_x[k], to_x[k] * 2 + c)
 
 
 def meet_all():
@@ -111,7 +103,6 @@
 
 def reciprocal(value):
     guess = pltpu.reciprocal(value, approx=True)
-    guess = guess * (2.0 - value * guess)
     return guess * (2.0 - value * guess)
 
 
@@ -132,11 +123,11 @@
         re = e[STRIP * strip : STRIP * (strip + 1)]
         alpha = jnp.zeros((STRIP, n), F32)
         beta = jnp.zeros((STRIP, n), F32)
-        for panel in range(STRIP // 8):
-            base = STRIP * strip + 8 * panel
-            c = [jnp.broadcast_to(ra[:, base + j : base + j + 1], (STRIP, n)) for j in range(8)]
-            for pair in range(4):
-                k = 8 * panel + 2 * pair
+        for panel in range(STRIP // PANEL):
+            base = STRIP * strip + PANEL * panel
+            c = [jnp.broadcast_to(ra[:, base + j : base + j + 1], (STRIP, n)) for j in range(PANEL)]
+            for pair in range(PANEL // 2):
+                k = PANEL * panel + 2 * pair
                 c0, c1 = c[2 * pair], c[2 * pair + 1]
                 p00, p01, p11 = c0[k : k + 1], c1[k : k + 1], c1[k + 1 : k + 2]
                 det = p00 * p11 - p01 * p01
@@ -144,7 +135,7 @@
                 below = local > k + 1
                 m0 = jnp.where(below, (c0 * p11 - c1 * p01) * inv, 0.0)
                 m1 = jnp.where(below, (c1 * p00 - c0 * p01) * inv, 0.0)
-                for j in range(2 * pair + 2, 8):
+                for j in range(2 * pair + 2, PANEL):
                     c[j] = c[j] - m0 * c[j][k : k + 1] - m1 * c[j][k + 1 : k + 2]
                 if k + 2 < STRIP:
                     ra = ra - m0 * ra[k : k + 1] - m1 * ra[k + 1 : k + 2]
@@ -170,20 +161,22 @@
     field, start, basis, gram_y,
     landed, high, low, both, cross,
     half_gram, pair_gram, sum_gram, parts_gram, all_gram, gram_x,
-    core_high, core_low, give, keep, pair_y, parts_y,
-    field_send, field_recv, gram_send, gram_recv, y_send, y_recv,
+    core, core_t, give, keep, pair_y,
+    plane_y, line_y, line_sum, plane_sum, upper_y, lower_y,
+    field_send, field_recv, gram_send, gram_recv, pair_send, pair_recv, y_send, y_recv,
 ):
     gx, yz, z, y, x, c = position()
     chip = gx * 4 + x
     meet_all()
 
     own = pl.ds(pl.multiple_of(yz * 512 + gx * 32, 32), 32)
-    for r in range(ROUNDS):
+
+    def exchange(r, carry):
         pltpu.make_async_copy(
             field.at[:, (gx * 8 + yz) * ROUNDS + r], landed.at[r, own], field_recv.at[r]
         ).start()
         each_other_device(
-            lambda to_gx, to_yz, r=r: send_to(
+            lambda to_gx, to_yz: send_to(
                 field.at[:, (to_gx * 8 + to_yz) * ROUNDS + r],
                 landed.at[r, own],
                 field_send.at[r],
@@ -192,6 +185,9 @@
                 to_yz,
             )
         )
+        return carry
+
+    lax.fori_loop(0, ROUNDS, exchange, 0)
 
     for r in range(ROUNDS):
         wait_for(landed.at[r], field_recv.at[r])
@@ -241,46 +237,70 @@
     total = jnp.concatenate([all_gram[512 * j : 512 * (j + 1), :] for j in range(4)], axis=1)
     gram_x[...] = (total + total.T) * (1.0 / (512 * 1024))
 
-    basis[...] = start[...]
-
-    def iterate(step, carry):
-        product = dot_exact(gram_x[...], basis[...], NN)
-        basis[...] = dot_exact(product, inverse_factor(dot_exact(product, product, TN)), NT)
-        return carry
-
-    lax.fori_loop(0, ITERS, iterate, 0)
-
-    b_high, b_low = split(basis[...].T)
+    def normaliser(product):
+        return inverse_factor(dot_exact(product, product, NT))
+
+    def iterate(step, product):
+        ahead = dot_exact(product, gram_x[...], NN)
+        return dot_exact(normaliser(product), ahead, NN)
+
+    product = dot_exact(start[...].T, gram_x[...], NN)
+    product = lax.fori_loop(0, ITERS - 1, iterate, product)
+    rows = dot_exact(normaliser(product), product, NN)
+    basis[...] = rows.T
+
+    b_high, b_low = split(rows)
     for r in range(ROUNDS):
         h, l = high[r], low[r]
         part = dot(b_high, h, NN) + (dot(b_high, l, NN) + dot(b_low, h, NN))
-        core_high[RANK * r : RANK * (r + 1), :], core_low[RANK * r : RANK * (r + 1), :] = split(part)
-
-    def columns_of(parity, j):
-        at = pl.ds(pl.multiple_of((2 * j + parity) * 128, 128), 128)
-        h, l = core_high[:, at], core_low[:, at]
-        return dot(core_high[...], h, TN) + (dot(core_high[...], l, TN) + dot(core_low[...], h, TN))
-
-    for j in range(4):
-        give[j] = columns_of(1 - c, j)
-        send_to(give.at[j], pair_y.at[j], y_send.at[j], y_recv.at[j], gx, partner)
-    for j in range(4):
-        keep[j] = columns_of(c, j)
-    for j in range(4):
-        wait_for(pair_y.at[j], y_recv.at[j])
-        keep[j] = keep[j] + pair_y[j]
-
-    def piece_y(to_gx, to_x):
-        return keep.at[to_x, pl.ds(pl.multiple_of(to_gx * 64, 64), 64)]
-
-    each_other_chip(
-        lambda to_gx, to_x, to_yz: send_to(
-            piece_y(to_gx, to_x), parts_y.at[chip], y_send.at[4], y_recv.at[4], to_gx, to_yz
-        )
-    )
-    parts_y[chip] = piece_y(gx, x)[...]
-    wait_for(parts_y.at[pl.ds(0, 63)], y_recv.at[4])
-    gram_y[...] = (jnp.sum(parts_y[...], axis=0) * (1.0 / 65536)).T
+        h, l = split(part)
+        for n, piece in enumerate((h, l, h)):
+            core[512 * n + RANK * r : 512 * n + RANK * (r + 1), :] = piece
+        h, l = split(part.T)
+        for n, piece in enumerate((h, h, l)):
+            core_t[:, 512 * n + RANK * r : 512 * n + RANK * (r + 1)] = piece
+
+    def columns_of(parity, block, n):
+        pair = [core[:, pl.ds(pl.multiple_of((2 * j + parity) * 128, 128), 128)] for j in (2 * n, 2 * n + 1)]
+        value = dot(core_t[...], jnp.concatenate(pair, axis=1), NN)
+        block[2 * n] = value[:, :128].reshape(16, 64, 128)
+        block[2 * n + 1] = value[:, 128:].reshape(16, 64, 128)
+
+    for n in range(2):
+        columns_of(1 - c, give, n)
+        pair_half = pair_y.at[pl.ds(2 * n, 2)]
+        send_to(give.at[pl.ds(2 * n, 2)], pair_half, pair_send.at[n], pair_recv.at[n], gx, partner)
+    for n in range(2):
+        columns_of(c, keep, n)
+    for n in range(2):
+        wait_for(pair_y.at[pl.ds(2 * n, 2)], pair_recv.at[n])
+        keep[2 * n : 2 * n + 2] = keep[2 * n : 2 * n + 2] + pair_y[2 * n : 2 * n + 2]
+
+    to_gx, to_x = routes()
+    plane = [to_gx[i][(a + i) % 4] for a in range(4) for i in range(4)][1:]
+
+    first, second = pl.ds(0, 32), pl.ds(32, 32)
+    for n, at in enumerate(plane):
+        send_to(keep.at[:, at, second], plane_y.at[gx], y_send.at[0], y_recv.at[0], at, yz)
+        if n % 5 == 0:
+            to = to_x[1 + n // 5]
+            send_to(keep.at[to, :, first], line_y.at[x], y_send.at[1], y_recv.at[1], gx, 2 * to + c)
+    plane_y[gx] = keep[:, gx, 32:, :]
+    line_y[x] = keep[x, :, :32, :]
+    wait_for(line_y.at[pl.ds(0, 3)], y_recv.at[1])
+    line_sum[...] = jnp.sum(line_y[...], axis=0)
+    for at in plane:
+        send_to(line_sum.at[at], upper_y.at[gx], y_send.at[2], y_recv.at[2], at, yz)
+    wait_for(plane_y.at[pl.ds(0, 15)], y_recv.at[0])
+    plane_sum[...] = jnp.sum(plane_y[...], axis=0)
+    for at in to_x[1:]:
+        send_to(plane_sum.at[at], lower_y.at[x], y_send.at[3], y_recv.at[3], gx, 2 * at + c)
+    upper_y[gx] = line_sum[gx]
+    lower_y[x] = plane_sum[x]
+    wait_for(upper_y.at[pl.ds(0, 15)], y_recv.at[2])
+    wait_for(lower_y.at[pl.ds(0, 3)], y_recv.at[3])
+    gram_y[0:32, :] = jnp.sum(upper_y[...], axis=0) * (1.0 / 65536)
+    gram_y[32:64, :] = jnp.sum(lower_y[...], axis=0) * (1.0 / 65536)
 
     for r in range(ROUNDS):
         wait_for(landed.at[r, pl.ds(0, 127 * 32)], field_send.at[r])
@@ -288,18 +308,21 @@
     wait_for(parts_gram.at[pl.ds(0, 63)], gram_send.at[1])
     wait_for(parts_gram.at[pl.ds(0, 63)], gram_send.at[2])
     wait_for(all_gram.at[mine], gram_send.at[3])
-    for j in range(4):
-        wait_for(give.at[j], y_send.at[j])
-    wait_for(parts_y.at[pl.ds(0, 63)], y_send.at[4])
+    for n in range(2):
+        wait_for(give.at[pl.ds(2 * n, 2)], pair_send.at[n])
+    wait_for(plane_y.at[pl.ds(0, 15)], y_send.at[0])
+    wait_for(line_y.at[pl.ds(0, 3)], y_send.at[1])
+    wait_for(upper_y.at[pl.ds(0, 15)], y_send.at[2])
+    wait_for(lower_y.at[pl.ds(0, 3)], y_send.at[3])
 
 
 def on_device(field, start):
     vmem = pl.BlockSpec(memory_space=pltpu.VMEM)
-    return pl.pallas_call(
+    basis, piece = pl.pallas_call(
         kernel,
         out_shape=(
             jax.ShapeDtypeStruct((512, RANK), F32),
-            jax.ShapeDtypeStruct((128, 64), F32),
+            jax.ShapeDtypeStruct((64, 128), F32),
         ),
         in_specs=[pl.BlockSpec(memory_space=pl.ANY), vmem],
         out_specs=(vmem, vmem),
@@ -315,23 +338,31 @@
             pltpu.VMEM((64, 16, 128), F32),
             pltpu.VMEM((2048, 128), F32),
             pltpu.VMEM((512, 512), F32),
-            pltpu.VMEM((512, 1024), BF16),
-            pltpu.VMEM((512, 1024), BF16),
-            pltpu.VMEM((4, 1024, 128), F32),
-            pltpu.VMEM((4, 1024, 128), F32),
-            pltpu.VMEM((4, 1024, 128), F32),
-            pltpu.VMEM((64, 64, 128), F32),
+            pltpu.VMEM((1536, 1024), BF16),
+            pltpu.VMEM((1024, 1536), BF16),
+            pltpu.VMEM((4, 16, 64, 128), F32),
+            pltpu.VMEM((4, 16, 64, 128), F32),
+            pltpu.VMEM((4, 16, 64, 128), F32),
+            pltpu.VMEM((16, 4, 32, 128), F32),
+            pltpu.VMEM((4, 16, 32, 128), F32),
+            pltpu.VMEM((16, 32, 128), F32),
+            pltpu.VMEM((4, 32, 128), F32),
+            pltpu.VMEM((16, 32, 128), F32),
+            pltpu.VMEM((4, 32, 128), F32),
             pltpu.SemaphoreType.DMA((ROUNDS,)),
             pltpu.SemaphoreType.DMA((ROUNDS,)),
             pltpu.SemaphoreType.DMA((4,)),
             pltpu.SemaphoreType.DMA((4,)),
-            pltpu.SemaphoreType.DMA((5,)),
-            pltpu.SemaphoreType.DMA((5,)),
+            pltpu.SemaphoreType.DMA((2,)),
+            pltpu.SemaphoreType.DMA((2,)),
+            pltpu.SemaphoreType.DMA((4,)),
+            pltpu.SemaphoreType.DMA((4,)),
         ],
         compiler_params=pltpu.CompilerParams(
             collective_id=0, has_side_effects=True, vmem_limit_bytes=56 << 20
         ),
     )(field, start)
+    return basis, piece.T
 
 
 def solution(mesh):

time: 209 us -> 183 us (0.88)
  Pallas kernels: 203 us -> 179 us
    pallas_call x1, Pallas kernels: 203 us -> 179 us  [on_device(): pl.pallas_call(kernel, out_shape=(jax.ShapeDtypeStruct((512, RANK), F32),...]
where the time goes in v2:
time: 183 us; the launch traced here: 182 us
  Pallas kernels  179 us (98%)
  local copies, waits for them, and re-layouts  3.04 us (2%)
    pallas_call x1, Pallas kernels, on_device(): pl.pallas_call(kernel, out_shape=(jax.ShapeDtypeStruct((512, RANK), F32),...  179 us

profile of v2, /device:TPU:0, one launch (start us, length us, event | category | flops | bytes accessed | tf_op | source)
XLA Modules:
  0.0 182.3 jit_solution(15162021312643262852)
XLA Ops:
  0.6 178.6 %shard_map.41 = (f32[512,128]{1,0:T(8,128)}, f32[64,128]{1,0:T(8,128)}) custom-call(f32[32,512,128]{2,1,0:T(8,128)} %field.1, f32[512,128]{1,0:T(8,128)} %start.1), custom_call_target="tpu_custom_call" | custom-call | tf_op jit(solution)/shard_map/pallas_call | solution.py:321
  179.2 1.7 copy.6
  180.9 1.4 copy.7

commit v3 on v2

--- a/solution.py
+++ b/solution.py
@@ -18,6 +18,7 @@
 NN = (((1,), (0,)), ((), ()))
 NT = (((1,), (1,)), ((), ()))
 TN = (((0,), (0,)), ((), ()))
+BLOCKS = [(0, 0), (1, 0), (2, 0), (3, 0), (1, 1), (2, 1), (3, 1), (2, 2), (3, 2), (3, 3)]
 
 
 def dot(left, right, dims, precision=None):
@@ -73,7 +74,7 @@
     to_gx, to_x = routes()
     c = lax.axis_index("yz") % 2
     for i, j, k in CHIP_STEPS[1:]:
-        action(to_gx[i][j], to_x[k], to_x[k] * 2 + c)
+        action((i, j, k), to_gx[i][j], to_x[k], to_x[k] * 2 + c)
 
 
 def meet_all():
@@ -99,11 +100,6 @@
 
 def wait_for(ref, sem):
     pltpu.make_async_copy(ref, ref, sem).wait()
-
-
-def reciprocal(value):
-    guess = pltpu.reciprocal(value, approx=True)
-    return guess * (2.0 - value * guess)
 
 
 def inverse_factor(cross):
@@ -131,11 +127,14 @@
                 c0, c1 = c[2 * pair], c[2 * pair + 1]
                 p00, p01, p11 = c0[k : k + 1], c1[k : k + 1], c1[k + 1 : k + 2]
                 det = p00 * p11 - p01 * p01
-                inv = reciprocal(det)
+                inv = pltpu.reciprocal(det, approx=True)
                 below = local > k + 1
-                m0 = jnp.where(below, (c0 * p11 - c1 * p01) * inv, 0.0)
-                m1 = jnp.where(below, (c1 * p00 - c0 * p01) * inv, 0.0)
-                for j in range(2 * pair + 2, PANEL):
+                n0 = jnp.where(below, c0 * p11 - c1 * p01, 0.0)
+                n1 = jnp.where(below, c1 * p00 - c0 * p01, 0.0)
+                m0, m1 = n0 * inv, n1 * inv
+                for j in range(2 * pair + 2, min(2 * pair + 4, PANEL)):
+                    c[j] = c[j] - (n0 * c[j][k : k + 1] + n1 * c[j][k + 1 : k + 2]) * inv
+                for j in range(2 * pair + 4, PANEL):
                     c[j] = c[j] - m0 * c[j][k : k + 1] - m1 * c[j][k + 1 : k + 2]
                 if k + 2 < STRIP:
                     ra = ra - m0 * ra[k : k + 1] - m1 * ra[k + 1 : k + 2]
@@ -159,8 +158,8 @@
 
 def kernel(
     field, start, basis, gram_y,
-    landed, high, low, both, cross,
-    half_gram, pair_gram, sum_gram, parts_gram, all_gram, gram_x,
+    landed, high, low, left_half, right_half,
+    own_gram, pair_gram, sum_gram, parts_gram, all_gram, gram_x,
     core, core_t, give, keep, pair_y,
     plane_y, line_y, line_sum, plane_sum, upper_y, lower_y,
     field_send, field_recv, gram_send, gram_recv, pair_send, pair_recv, y_send, y_recv,
@@ -196,46 +195,72 @@
             high[r, :, 128 * j : 128 * (j + 1)] = h
             low[r, :, 128 * j : 128 * (j + 1)] = l
         h, l = high[r], low[r]
+        left = jnp.concatenate([h, h, l], axis=1)
+        right = jnp.concatenate([h, l, h], axis=1)
         if r == 0:
-            both[...] = dot(h, h, NT)
-            cross[...] = dot(h, l, NT)
+            left_half[...] = dot(left, right[:256], NT)
+            right_half[...] = dot(left[256:], right[256:], NT)
         else:
-            both[...] += dot(h, h, NT)
-            cross[...] += dot(h, l, NT)
-    for j in range(4):
-        columns = slice(128 * j, 128 * (j + 1))
-        half_gram[512 * j : 512 * (j + 1), :] = 0.5 * both[:, columns] + cross[:, columns]
-
-    mine = pl.ds(pl.multiple_of(c * 1024, 1024), 1024)
-    other = pl.ds(pl.multiple_of((1 - c) * 1024, 1024), 1024)
+            left_half[...] += dot(left, right[:256], NT)
+            right_half[...] += dot(left[256:], right[256:], NT)
+    for n, (i, j) in enumerate(BLOCKS):
+        if j < 2:
+            block = left_half[128 * i : 128 * (i + 1), 128 * j : 128 * (j + 1)]
+        else:
+            block = right_half[128 * (i - 2) : 128 * (i - 1), 128 * (j - 2) : 128 * (j - 1)]
+        own_gram[128 * n : 128 * (n + 1), :] = block
+
+    def half(of):
+        return pl.ds(pl.multiple_of(of * 640, 128), 640)
+
+    def rows_of(at, place, size):
+        start = at * 40 + jnp.where(place == 0, 0, 8 + 8 * place)
+        return pl.ds(pl.multiple_of(start, 8), size)
+
+    place = (x + 8 - z - y) % 4
+    wide = place == 0
     partner = x * 2 + 1 - c
-    send_to(half_gram.at[other], pair_gram, gram_send.at[0], gram_recv.at[0], gx, partner)
+    send_to(own_gram.at[half(1 - c)], pair_gram, gram_send.at[0], gram_recv.at[0], gx, partner)
     wait_for(pair_gram, gram_recv.at[0])
-    sum_gram[...] = half_gram[mine, :] + pair_gram[...]
-    each_other_chip(
-        lambda to_gx, to_x, to_yz: send_to(
-            sum_gram.at[pl.ds(pl.multiple_of((to_gx * 4 + to_x) * 16, 16), 16)],
-            parts_gram.at[chip],
-            gram_send.at[1],
-            gram_recv.at[1],
-            to_gx,
-            to_yz,
+    sum_gram[...] = own_gram[half(c), :] + pair_gram[...]
+    places = [(place + (1 + 2 * c) * n) % 4 for n in range(4)]
+
+    def scatter(steps, to_gx, to_x, to_yz):
+        to_place = places[(steps[2] - steps[0] - steps[1]) % 4]
+
+        def part(size):
+            send_to(
+                sum_gram.at[rows_of(to_gx, to_place, size)], parts_gram.at[chip, pl.ds(0, size)],
+                gram_send.at[1], gram_recv.at[1], to_gx, to_yz,
+            )
+
+        pl.when(to_place == 0)(lambda: part(16))
+        pl.when(to_place != 0)(lambda: part(8))
+
+    each_other_chip(scatter)
+
+    def finish(size):
+        mine = rows_of(gx, place, size)
+        parts_gram[chip, 0:size] = sum_gram[mine, :]
+        wait_for(parts_gram.at[pl.ds(0, 63), pl.ds(0, size)], gram_recv.at[1])
+        piece = pl.ds(pl.multiple_of(c * 640 + mine.start, 8), size)
+        all_gram[piece, :] = jnp.sum(parts_gram[:, 0:size], axis=0)
+        each_other_chip(
+            lambda steps, to_gx, to_x, to_yz: send_to(
+                all_gram.at[piece], all_gram.at[piece], gram_send.at[2], gram_recv.at[2], to_gx, to_yz
+            )
         )
-    )
-    parts_gram[chip] = sum_gram[pl.ds(pl.multiple_of(chip * 16, 16), 16), :]
-    wait_for(parts_gram.at[pl.ds(0, 63)], gram_recv.at[1])
-    piece = pl.ds(pl.multiple_of(c * 1024 + chip * 16, 16), 16)
-    all_gram[piece, :] = jnp.sum(parts_gram[...], axis=0)
-    each_other_chip(
-        lambda to_gx, to_x, to_yz: send_to(
-            all_gram.at[piece], all_gram.at[piece], gram_send.at[2], gram_recv.at[2], to_gx, to_yz
-        )
-    )
-    wait_for(all_gram.at[pl.ds(0, 63 * 16)], gram_recv.at[2])
-    send_to(all_gram.at[mine], all_gram.at[mine], gram_send.at[3], gram_recv.at[3], gx, partner)
-    wait_for(all_gram.at[other], gram_recv.at[3])
-    total = jnp.concatenate([all_gram[512 * j : 512 * (j + 1), :] for j in range(4)], axis=1)
-    gram_x[...] = (total + total.T) * (1.0 / (512 * 1024))
+        wait_for(all_gram.at[pl.ds(0, 640 - size)], gram_recv.at[2])
+
+    pl.when(wide)(lambda: finish(16))
+    pl.when(jnp.logical_not(wide))(lambda: finish(8))
+    send_to(all_gram.at[half(c)], all_gram.at[half(c)], gram_send.at[3], gram_recv.at[3], gx, partner)
+    wait_for(all_gram.at[half(1 - c)], gram_recv.at[3])
+    for n, (i, j) in enumerate(BLOCKS):
+        block = all_gram[128 * n : 128 * (n + 1), :] * (1.0 / (512 * 1024))
+        gram_x[128 * i : 128 * (i + 1), 128 * j : 128 * (j + 1)] = block
+        if i != j:
+            gram_x[128 * j : 128 * (j + 1), 128 * i : 128 * (i + 1)] = block.T
 
     def normaliser(product):
         return inverse_factor(dot_exact(product, product, NT))
@@ -305,15 +330,22 @@
     for r in range(ROUNDS):
         wait_for(landed.at[r, pl.ds(0, 127 * 32)], field_send.at[r])
     wait_for(pair_gram, gram_send.at[0])
-    wait_for(parts_gram.at[pl.ds(0, 63)], gram_send.at[1])
-    wait_for(parts_gram.at[pl.ds(0, 63)], gram_send.at[2])
-    wait_for(all_gram.at[mine], gram_send.at[3])
+    pl.when(wide)(lambda: wait_for(own_gram.at[pl.ds(0, 15 * 16 + 48 * 8)], gram_send.at[1]))
+    pl.when(jnp.logical_not(wide))(lambda: wait_for(own_gram.at[pl.ds(0, 16 * 16 + 47 * 8)], gram_send.at[1]))
+    pl.when(wide)(lambda: wait_for(parts_gram.at[pl.ds(0, 63)], gram_send.at[2]))
+    pl.when(jnp.logical_not(wide))(lambda: wait_for(parts_gram.at[pl.ds(0, 63), pl.ds(0, 8)], gram_send.at[2]))
+    wait_for(all_gram.at[half(c)], gram_send.at[3])
     for n in range(2):
         wait_for(give.at[pl.ds(2 * n, 2)], pair_send.at[n])
     wait_for(plane_y.at[pl.ds(0, 15)], y_send.at[0])
     wait_for(line_y.at[pl.ds(0, 3)], y_send.at[1])
     wait_for(upper_y.at[pl.ds(0, 15)], y_send.at[2])
     wait_for(lower_y.at[pl.ds(0, 3)], y_send.at[3])
+
+
+def deliver(basis, piece, basis_out, piece_out):
+    basis_out[...] = basis[...]
+    piece_out[...] = piece[...]
 
 
 def on_device(field, start):
@@ -330,13 +362,13 @@
             pltpu.VMEM((ROUNDS, 4096, 128), F32),
             pltpu.VMEM((ROUNDS, 512, 1024), BF16),
             pltpu.VMEM((ROUNDS, 512, 1024), BF16),
-            pltpu.VMEM((512, 512), F32),
-            pltpu.VMEM((512, 512), F32),
-            pltpu.VMEM((2048, 128), F32),
-            pltpu.VMEM((1024, 128), F32),
-            pltpu.VMEM((1024, 128), F32),
+            pltpu.VMEM((512, 256), F32),
+            pltpu.VMEM((256, 256), F32),
+            pltpu.VMEM((1280, 128), F32),
+            pltpu.VMEM((640, 128), F32),
+            pltpu.VMEM((640, 128), F32),
             pltpu.VMEM((64, 16, 128), F32),
-            pltpu.VMEM((2048, 128), F32),
+            pltpu.VMEM((1280, 128), F32),
             pltpu.VMEM((512, 512), F32),
             pltpu.VMEM((1536, 1024), BF16),
             pltpu.VMEM((1024, 1536), BF16),
@@ -362,6 +394,15 @@
             collective_id=0, has_side_effects=True, vmem_limit_bytes=56 << 20
         ),
     )(field, start)
+    basis, piece = pl.pallas_call(
+        deliver,
+        out_shape=(
+            jax.ShapeDtypeStruct((512, RANK), F32),
+            jax.ShapeDtypeStruct((64, 128), F32),
+        ),
+        in_specs=[vmem, vmem],
+        out_specs=(vmem, vmem),
+    )(basis, piece)
     return basis, piece.T
 
 

time: 183 us -> 178 us (0.973)
  local copies, waits for them, and re-layouts: 3.04 us -> 0 us
  Pallas kernels: 179 us -> 177 us
    pallas_call x1, Pallas kernels: 179 us -> 175 us  [on_device(): pl.pallas_call(kernel, out_shape=(jax.ShapeDtypeStruct((512, RANK), F32),...]
    unnamed x2 -> x0, local copies, waits for them, and re-layouts: 3.04 us -> none
where the time goes in v3:
time: 178 us
  Pallas kernels  177 us (99%)
    pallas_call x1, Pallas kernels, on_device(): pl.pallas_call(kernel, out_shape=(jax.ShapeDtypeStruct((512, RANK), F32),...  175 us

profile of v3, /device:TPU:0, one launch (start us, length us, event | category | flops | bytes accessed | tf_op | source)
XLA Modules:
  0.0 177.7 jit_solution(9659681991437766257)
XLA Ops:
  0.6 175.4 %shard_map.41 = (f32[512,128]{1,0:T(8,128)}, f32[64,128]{1,0:T(8,128)}) custom-call(f32[32,512,128]{2,1,0:T(8,128)} %field.1, f32[512,128]{1,0:T(8,128)} %start.1), custom_call_target="tpu_custom_call" | custom-call | tf_op jit(solution)/shard_map/pallas_call | solution.py:353
  176.0 1.7 shard_map.42

commit v4 on v3

--- a/solution.py
+++ b/solution.py
@@ -38,6 +38,22 @@
     high = value.astype(BF16)
     rest = value - high.astype(F32)
     return (high,) + split(rest)
+
+
+def stacked(value, order, axis):
+    parts = split3(value)
+    return jnp.concatenate([parts[n] for n in order], axis=axis)
+
+
+def dot_six(left, right):
+    return dot(stacked(left, (0, 0, 1, 0, 1, 2), 1), stacked(right, (0, 1, 0, 2, 1, 0), 0), NN)
+
+
+def row_gram(value):
+    high, middle, low = split3(value)
+    mixed = dot(high, middle, NT) + dot(high, low, NT)
+    both = jnp.concatenate([high, middle], axis=1)
+    return dot(both, both, NT) + (mixed + mixed.T)
 
 
 def position():
@@ -147,9 +163,8 @@
         ue = alpha * (re - beta * pltpu.roll(re, 1, 0))
         done.append(ue)
         if strip + 1 < n // STRIP:
-            h, m, l = split3(jnp.concatenate([ua, ue], axis=1))
-            left = jnp.concatenate([part[:, :n] for part in (h, h, m, h, m, l)], axis=0)
-            right = jnp.concatenate([h, m, h, l, m, h], axis=0)
+            left = stacked(ua, (0, 0, 1, 0, 1, 2), 0)
+            right = stacked(jnp.concatenate([ua, ue], axis=1), (0, 1, 0, 2, 1, 0), 0)
             update = dot(left, right, TN)
             a = a - update[:, :n]
             e = e - update[:, n:]
@@ -263,15 +278,15 @@
             gram_x[128 * j : 128 * (j + 1), 128 * i : 128 * (i + 1)] = block.T
 
     def normaliser(product):
-        return inverse_factor(dot_exact(product, product, NT))
+        return inverse_factor(row_gram(product))
 
     def iterate(step, product):
         ahead = dot_exact(product, gram_x[...], NN)
-        return dot_exact(normaliser(product), ahead, NN)
+        return dot_six(normaliser(product), ahead)
 
     product = dot_exact(start[...].T, gram_x[...], NN)
     product = lax.fori_loop(0, ITERS - 1, iterate, product)
-    rows = dot_exact(normaliser(product), product, NN)
+    rows = dot_six(normaliser(product), product)
     basis[...] = rows.T
 
     b_high, b_low = split(rows)
@@ -285,21 +300,22 @@
         for n, piece in enumerate((h, h, l)):
             core_t[:, 512 * n + RANK * r : 512 * n + RANK * (r + 1)] = piece
 
-    def columns_of(parity, block, n):
+    def columns_of(parity, n):
         pair = [core[:, pl.ds(pl.multiple_of((2 * j + parity) * 128, 128), 128)] for j in (2 * n, 2 * n + 1)]
-        value = dot(core_t[...], jnp.concatenate(pair, axis=1), NN)
-        block[2 * n] = value[:, :128].reshape(16, 64, 128)
-        block[2 * n + 1] = value[:, 128:].reshape(16, 64, 128)
+        return dot(core_t[...], jnp.concatenate(pair, axis=1), NN)
 
     for n in range(2):
-        columns_of(1 - c, give, n)
-        pair_half = pair_y.at[pl.ds(2 * n, 2)]
-        send_to(give.at[pl.ds(2 * n, 2)], pair_half, pair_send.at[n], pair_recv.at[n], gx, partner)
+        value = columns_of(1 - c, n)
+        for j in range(2):
+            give[2 * n + j] = value[:, 128 * j : 128 * (j + 1)].reshape(16, 64, 128)
+        blocks = pl.ds(2 * n, 2)
+        send_to(give.at[blocks], pair_y.at[blocks], pair_send.at[n], pair_recv.at[n], gx, partner)
     for n in range(2):
-        columns_of(c, keep, n)
-    for n in range(2):
+        value = columns_of(c, n)
         wait_for(pair_y.at[pl.ds(2 * n, 2)], pair_recv.at[n])
-        keep[2 * n : 2 * n + 2] = keep[2 * n : 2 * n + 2] + pair_y[2 * n : 2 * n + 2]
+        for j in range(2):
+            block = value[:, 128 * j : 128 * (j + 1)].reshape(16, 64, 128)
+            keep[2 * n + j] = block + pair_y[2 * n + j]
 
     to_gx, to_x = routes()
     plane = [to_gx[i][(a + i) % 4] for a in range(4) for i in range(4)][1:]

time: 178 us -> 177 us (level)
  no operation moved by 1% of the time
where the time goes in v4:
time: 177 us; the launch traced here: 176 us
  Pallas kernels  176 us (99%)
    pallas_call x1, Pallas kernels, on_device(): pl.pallas_call(kernel, out_shape=(jax.ShapeDtypeStruct((512, RANK), F32),...  174 us

profile of v4, /device:TPU:0, one launch (start us, length us, event | category | flops | bytes accessed | tf_op | source)
XLA Modules:
  0.0 176.3 jit_solution(10568931974350992661)
XLA Ops:
  0.6 174.0 %shard_map.41 = (f32[512,128]{1,0:T(8,128)}, f32[64,128]{1,0:T(8,128)}) custom-call(f32[32,512,128]{2,1,0:T(8,128)} %field.1, f32[512,128]{1,0:T(8,128)} %start.1), custom_call_target="tpu_custom_call" | custom-call | tf_op jit(solution)/shard_map/pallas_call | solution.py:369
  174.6 1.7 shard_map.42

commit v5 on v4

--- a/solution.py
+++ b/solution.py
@@ -312,20 +312,20 @@
         send_to(give.at[blocks], pair_y.at[blocks], pair_send.at[n], pair_recv.at[n], gx, partner)
     for n in range(2):
         value = columns_of(c, n)
+        for j in range(2):
+            keep[2 * n + j] = value[:, 128 * j : 128 * (j + 1)].reshape(16, 64, 128)
+    for n in range(2):
         wait_for(pair_y.at[pl.ds(2 * n, 2)], pair_recv.at[n])
-        for j in range(2):
-            block = value[:, 128 * j : 128 * (j + 1)].reshape(16, 64, 128)
-            keep[2 * n + j] = block + pair_y[2 * n + j]
+        keep[2 * n : 2 * n + 2] = keep[2 * n : 2 * n + 2] + pair_y[2 * n : 2 * n + 2]
 
     to_gx, to_x = routes()
     plane = [to_gx[i][(a + i) % 4] for a in range(4) for i in range(4)][1:]
 
     first, second = pl.ds(0, 32), pl.ds(32, 32)
-    for n, at in enumerate(plane):
+    for to in to_x[1:]:
+        send_to(keep.at[to, :, first], line_y.at[x], y_send.at[1], y_recv.at[1], gx, 2 * to + c)
+    for at in plane:
         send_to(keep.at[:, at, second], plane_y.at[gx], y_send.at[0], y_recv.at[0], at, yz)
-        if n % 5 == 0:
-            to = to_x[1 + n // 5]
-            send_to(keep.at[to, :, first], line_y.at[x], y_send.at[1], y_recv.at[1], gx, 2 * to + c)
     plane_y[gx] = keep[:, gx, 32:, :]
     line_y[x] = keep[x, :, :32, :]
     wait_for(line_y.at[pl.ds(0, 3)], y_recv.at[1])

time: 177 us -> 176 us (level)
  no operation moved by 1% of the time
where the time goes in v5:
time: 176 us
  Pallas kernels  175 us (99%)
    pallas_call x1, Pallas kernels, on_device(): pl.pallas_call(kernel, out_shape=(jax.ShapeDtypeStruct((512, RANK), F32),...  174 us

profile of v5, /device:TPU:0, one launch (start us, length us, event | category | flops | bytes accessed | tf_op | source)
XLA Modules:
  0.0 175.8 jit_solution(7601653460724543591)
XLA Ops:
  0.6 173.5 %shard_map.41 = (f32[512,128]{1,0:T(8,128)}, f32[64,128]{1,0:T(8,128)}) custom-call(f32[32,512,128]{2,1,0:T(8,128)} %field.1, f32[512,128]{1,0:T(8,128)} %start.1), custom_call_target="tpu_custom_call" | custom-call | tf_op jit(solution)/shard_map/pallas_call | solution.py:369
  174.2 1.7 shard_map.42

commit v6 on v5

--- a/solution.py
+++ b/solution.py
@@ -68,7 +68,7 @@
     return [[to_z[i] * 4 + to_y[j] for j in range(4)] for i in range(4)], to_x
 
 
-CHIP_STEPS = [(i, (a + i) % 4, (b + i) % 4) for b in range(4) for a in range(4) for i in range(4)]
+CHIP_STEPS = [(i, (a + 3 * i) % 4, (b + i) % 4) for b in range(4) for a in range(4) for i in range(4)]
 
 
 def each_other_device(action):

time: 176 us -> 176 us (level)
  no operation moved by 1% of the time
where the time goes in v6:
time: 176 us
  Pallas kernels  175 us (99%)
    pallas_call x1, Pallas kernels, on_device(): pl.pallas_call(kernel, out_shape=(jax.ShapeDtypeStruct((512, RANK), F32),...  173 us

profile of v6, /device:TPU:0, one launch (start us, length us, event | category | flops | bytes accessed | tf_op | source)
XLA Modules:
  0.0 175.8 jit_solution(15499926157690060441)
XLA Ops:
  0.6 173.5 %shard_map.41 = (f32[512,128]{1,0:T(8,128)}, f32[64,128]{1,0:T(8,128)}) custom-call(f32[32,512,128]{2,1,0:T(8,128)} %field.1, f32[512,128]{1,0:T(8,128)} %start.1), custom_call_target="tpu_custom_call" | custom-call | tf_op jit(solution)/shard_map/pallas_call | solution.py:369
  174.1 1.7 shard_map.42
